TPU v7x, 512 devices: a whole 4x4x16 slice. The times are simulated.
512 devices in a mesh: dp: 8 (over y, core), expert: 64 (over x, z).
Axes of the slice: x: 4, y: 4, z: 16, core: 2. Of those that a mesh axis runs over, the one named last changes fastest.
Arguments:
- activations: bfloat16 [1024, 8, 1536], P('expert', None, 'dp'), may hold values from -6 to 6
- w_down: bfloat16 [64, 1536, 4096], P('expert', 'dp'), may hold values from -0.15625 to 0.15625
- gate_weights: float32 [1024, 8], P('expert'), may hold values from 0.05 to 1
- cotangent: bfloat16 [1024, 4096], P('expert', 'dp'), may hold values from -0.59765625 to 0.59765625
- expert_ids: int32 [1024, 8], P('expert'), may hold values from 0 to 63, as said below
- replica_pick: int32 [1024, 8], P('expert'), may hold values from 0 to 1, as said below
- placement: int32 [16, 2], replicated, may hold values from 0 to 63, as said below
- group_cap: int32 [64], replicated, may hold values from 1 to 3, as said below
Outputs:
- combined: bfloat16 [1024, 4096], P('expert', 'dp')
- act_grad: bfloat16 [1024, 8, 1536], P('expert', None, 'dp')
- weight_grad: bfloat16 [64, 1536, 4096], P('expert', 'dp')
- gate_grad: float32 [1024, 8], P('expert')
Inputs may be any that keep to these rules, and one draw needn't show every extreme that they name: `expert_ids`: each row names 8 different experts. One expert, drawn from the seed and without a replica, is named by every token; replicated experts are named more often than the others. `replica_pick`: read only for rows whose expert has a replica. `placement`: column 0 holds distinct experts, column 1 distinct indices of expert; no index hosts a replica of the expert it owns, and no expert owned by a host is itself replicated. `group_cap`: the expert named by every token has its owner's entry equal to 3.
All inputs are finite; a program needn't handle non-finite values.
Results may differ from a plain program's by a relative error of at most 0.02.
Values may be sent and summed in bfloat16 or wider, within the bound.
No kernel may reach another device: no remote copies, remote signals or barrier semaphores. Data moves between devices by JAX's collectives and lax.ppermute only.
A program may use at most 64 MiB of HBM per device.

v0:
```python
import jax
import jax.numpy as jnp
from jax import lax
from jax.sharding import PartitionSpec as P


def routing_table(block_ids, block_pick, placement, group_cap):
    n_dev = group_cap.shape[0]
    flat_ids = block_ids.reshape(-1)
    flat_pick = block_pick.reshape(-1)
    match_copy = (flat_ids[:, None] == placement[None, :, 0]).astype(jnp.int32)
    has_copy = jnp.sum(match_copy, axis=1, dtype=jnp.int32)
    host_dev = jnp.sum(match_copy * placement[None, :, 1], axis=1, dtype=jnp.int32)
    to_copy = (has_copy > 0) & (flat_pick == 1)
    destination = jnp.where(to_copy, host_dev, flat_ids)
    row_kind = jnp.where(to_copy, 2, 1).astype(jnp.int32)
    onehot_dest = (destination[:, None] == jnp.arange(n_dev, dtype=jnp.int32)[None, :]).astype(
        jnp.int32
    )
    earlier = jnp.cumsum(onehot_dest, axis=0, dtype=jnp.int32) - onehot_dest
    row_rank = jnp.sum(earlier * onehot_dest, axis=1, dtype=jnp.int32)
    row_limit = jnp.sum(onehot_dest * group_cap[None, :], axis=1, dtype=jnp.int32)
    row_kept = row_rank < row_limit
    return (destination, row_kind, row_rank, row_kept)


def hosted(placement, n_dev):
    at_dev = (placement[:, 1][:, None] == jnp.arange(n_dev, dtype=jnp.int32)[None, :]).astype(
        jnp.int32
    )
    has_at = jnp.sum(at_dev, axis=0, dtype=jnp.int32)
    rep_at = jnp.sum(at_dev * placement[:, 0][:, None], axis=0, dtype=jnp.int32)
    return (has_at, rep_at)


def on_device(
    activations, w_down, gate_weights, cotangent, expert_ids, replica_pick, placement, group_cap
):
    n_dev = lax.axis_size("expert")
    tok_count, top_count, hidden_part = activations.shape
    width = w_down.shape[2]
    capacity = min(tok_count, 3 * tok_count * top_count // (2 * n_dev))
    slot_count = n_dev * capacity
    row_count = tok_count * top_count
    destination, row_kind, row_rank, row_kept = routing_table(
        expert_ids, replica_pick, placement, group_cap
    )
    slot_index = jnp.where(row_kept, destination * capacity + row_rank, slot_count)
    row_numbers = jnp.arange(row_count, dtype=jnp.int32)
    inverse = (
        jnp.full((slot_count + 1,), -1, jnp.int32).at[slot_index].set(row_numbers)[:slot_count]
    )
    slot_valid = inverse >= 0
    slot_rows = jnp.maximum(inverse, 0)
    slot_kind = jnp.where(slot_valid, jnp.take(row_kind, slot_rows, axis=0), 0).reshape(
        n_dev, capacity
    )
    safe_slot = jnp.minimum(slot_index, slot_count - 1)

    def to_slots(values):
        return jnp.where(
            slot_valid[:, None], jnp.take(values, slot_rows, axis=0), jnp.zeros((), values.dtype)
        )

    def to_rows(values):
        return jnp.where(
            row_kept[:, None], jnp.take(values, safe_slot, axis=0), jnp.zeros((), values.dtype)
        )

    has_at, rep_at = hosted(placement, n_dev)
    my_index = lax.axis_index("expert")
    is_host = jnp.take(has_at, my_index) > 0
    choose = (
        (has_at[:, None] > 0) & (rep_at[:, None] == jnp.arange(n_dev, dtype=jnp.int32)[None, :])
    ).astype(jnp.bfloat16)
    local_w = w_down[0]
    pieces = lax.all_to_all(local_w[None], "expert", split_axis=2, concat_axis=0, tiled=True)
    outgoing = jnp.einsum("de,ehc->dhc", choose, pieces, preferred_element_type=jnp.float32).astype(
        jnp.bfloat16
    )
    copy_w = lax.all_to_all(outgoing, "expert", split_axis=0, concat_axis=2, tiled=True)[0]
    flat_act = activations.reshape(row_count, hidden_part)
    sent = to_slots(flat_act).reshape(n_dev, capacity, hidden_part)
    arrived, arrived_kind = (
        lax.all_to_all(sent, "expert", split_axis=0, concat_axis=0, tiled=True),
        lax.all_to_all(slot_kind, "expert", split_axis=0, concat_axis=0, tiled=True),
    )
    inputs = arrived.reshape(slot_count, hidden_part)
    slot_kinds = arrived_kind.reshape(slot_count)
    own_mask = (slot_kinds == 1)[:, None]
    copy_mask = (slot_kinds == 2)[:, None]
    own_in = jnp.where(own_mask, inputs, jnp.zeros_like(inputs))
    copy_in = jnp.where(copy_mask, inputs, jnp.zeros_like(inputs))

    def forward_both(operands):
        return jnp.dot(operands[0], local_w, preferred_element_type=jnp.float32) + jnp.dot(
            operands[1], copy_w, preferred_element_type=jnp.float32
        )

    def forward_owned(operands):
        return jnp.dot(operands[0], local_w, preferred_element_type=jnp.float32)

    partial_value = lax.cond(is_host, forward_both, forward_owned, (own_in, copy_in))
    cotangent_full = lax.all_gather(cotangent, "dp", axis=1, tiled=True)
    returned = lax.all_to_all(
        partial_value.astype(jnp.bfloat16).reshape(n_dev, capacity, width),
        "expert",
        split_axis=0,
        concat_axis=0,
        tiled=True,
    )
    row_values = (
        to_rows(returned.reshape(slot_count, width))
        .astype(jnp.float32)
        .reshape(tok_count, top_count, width)
    )
    mixed_part = jnp.sum(gate_weights[:, :, None] * row_values, axis=1)
    combined = lax.psum_scatter(
        mixed_part.astype(jnp.bfloat16), "dp", scatter_dimension=1, tiled=True
    )
    gate_part = jnp.sum(cotangent_full.astype(jnp.float32)[:, None, :] * row_values, axis=2)
    gate_grad = lax.psum(gate_part, "dp")
    grad_tok = (
        (gate_weights[:, :, None] * cotangent_full.astype(jnp.float32)[:, None, :])
        .astype(jnp.bfloat16)
        .reshape(row_count, width)
    )
    grad_sent = to_slots(grad_tok).reshape(n_dev, capacity, width)
    grad_in = lax.all_to_all(grad_sent, "expert", split_axis=0, concat_axis=0, tiled=True)
    grad_in = grad_in.reshape(slot_count, width)

    def backward_both(operand):
        back_own = lax.dot_general(
            operand, local_w, (((1,), (1,)), ((), ())), preferred_element_type=jnp.float32
        )
        back_copy = lax.dot_general(
            operand, copy_w, (((1,), (1,)), ((), ())), preferred_element_type=jnp.float32
        )
        return jnp.where(own_mask, back_own, jnp.where(copy_mask, back_copy, 0.0)).astype(
            jnp.bfloat16
        )

    def backward_owned(operand):
        back_own = lax.dot_general(
            operand, local_w, (((1,), (1,)), ((), ())), preferred_element_type=jnp.float32
        )
        return jnp.where(own_mask, back_own, 0.0).astype(jnp.bfloat16)

    input_back = lax.cond(is_host, backward_both, backward_owned, grad_in)
    returned_grads = lax.all_to_all(
        input_back.reshape(n_dev, capacity, hidden_part),
        "expert",
        split_axis=0,
        concat_axis=0,
        tiled=True,
    )
    act_grad = to_rows(returned_grads.reshape(slot_count, hidden_part)).reshape(
        tok_count, top_count, hidden_part
    )
    own_grad = lax.dot_general(
        own_in, grad_in, (((0,), (0,)), ((), ())), preferred_element_type=jnp.float32
    )

    def copy_product(operands):
        return lax.dot_general(
            operands[0], operands[1], (((0,), (0,)), ((), ())), preferred_element_type=jnp.float32
        ).astype(jnp.bfloat16)

    def copy_nothing(operands):
        return jnp.zeros((operands[0].shape[1], operands[1].shape[1]), jnp.bfloat16)

    copy_grad = lax.cond(is_host, copy_product, copy_nothing, (copy_in, grad_in))
    grad_pieces = lax.all_to_all(copy_grad[None], "expert", split_axis=2, concat_axis=0, tiled=True)
    homeward = jnp.einsum(
        "de,dhc->ehc", choose, grad_pieces, preferred_element_type=jnp.float32
    ).astype(jnp.bfloat16)
    home_grad = lax.all_to_all(homeward, "expert", split_axis=0, concat_axis=2, tiled=True)[0]
    weight_grad = (own_grad + home_grad.astype(jnp.float32)).astype(jnp.bfloat16)[None]
    return (combined, act_grad, weight_grad, gate_grad)


def solution(mesh):
    return jax.shard_map(
        on_device,
        mesh=mesh,
        in_specs=(
            P("expert", None, "dp"),
            P("expert", "dp", None),
            P("expert", None),
            P("expert", "dp"),
            P("expert", None),
            P("expert", None),
            P(),
            P(),
        ),
        out_specs=(
            P("expert", "dp"),
            P("expert", None, "dp"),
            P("expert", "dp", None),
            P("expert", None),
        ),
        check_vma=False,
    )
```

profile of v0, /device:TPU:14, one launch (start us, length us, event | category | flops | bytes accessed | tf_op | source)
XLA Modules:
  0.0 808.6 jit_solution(3717038787633869883)
XLA Ops:
  7.2 9.9 %copy.94 = bf16[1,192,4096]{1,0,2:T(2,128)(2,1)} copy(bf16[1,192,4096]{2,1,0:T(8,128)(2,1)} %param.15) | data formatting | bytes 3145728 | tf_op args[1]
  17.6 23.5 %reduce.14 = bf16[4096,192]{1,0:T(8,128)(2,1)S(1)} reduce(bf16[4096,1,192]{2,1,0:T(2,128)(2,1)} %bitcast.115, bf16[]{:T(256)} %broadcast.341), dimensions={1}, to_apply=%bitcast.90.reduce_sub_computation | reduce | bytes 3145730
  41.1 3.3 reshape.474
  44.5 18.9 %all-to-all-start.2 = ((bf16[64,2,6144]{2,1,0:T(2,128)(2,1)}), bf16[64,2,6144]{2,1,0:T(2,128)(2,1)S(1)}, u32[]{:S(2)}, u32[]{:S(2)}) async-start(bf16[64,2,6144]{2,1,0:T(2,128)(2,1)} %reshape.474), calls=%async_computation.2 | async-start | bytes 3145728 | tf_op jit(solution)/shard_map/all_to_all | solution.py:77
  64.8 0.6 fusion.36
  65.4 1.0 scatter_custom_fusion
  66.5 1.6 gather_fusion
  68.4 0.8 select_n.203
  69.1 1.0 gather_fusion.1
  70.3 0.9 select_select_fusion.1
  71.2 68.4 %all-to-all-done.2 = bf16[64,2,6144]{2,1,0:T(2,128)(2,1)S(1)} async-done(((bf16[64,2,6144]{2,1,0:T(2,128)(2,1)}), bf16[64,2,6144]{2,1,0:T(2,128)(2,1)S(1)}, u32[]{:S(2)}, u32[]{:S(2)}) %all-to-all-start.2) | async-done | bytes 1572896 | tf_op jit(solution)/shard_map/all_to_all | solution.py:77
  139.6 6.9 all-to-all-start
  146.5 7.2 reshape.475
  153.7 2.5 copy.114
  156.3 2.7 all-to-all-done
  159.0 13.0 %all-to-all-start.1 = ((bf16[64,3,192]{2,1,0:T(4,128)(2,1)}), bf16[64,3,192]{2,1,0:T(4,128)(2,1)S(1)}, u32[]{:S(2)}, u32[]{:S(2)}) async-start(bf16[64,3,192]{2,1,0:T(4,128)(2,1)} %select_select_fusion.1), calls=%async_computation.1 | async-start | bytes 262144 | tf_op jit(solution)/shard_map/all_to_all | solution.py:85
  172.0 1.7 fusion.11
  173.7 2.5 copy.97
  176.3 10.5 %all-to-all-done.1 = bf16[64,3,192]{2,1,0:T(4,128)(2,1)S(1)} async-done(((bf16[64,3,192]{2,1,0:T(4,128)(2,1)}), bf16[64,3,192]{2,1,0:T(4,128)(2,1)S(1)}, u32[]{:S(2)}, u32[]{:S(2)}) %all-to-all-start.1) | async-done | bytes 73760 | tf_op jit(solution)/shard_map/all_to_all | solution.py:85
  186.8 6.7 all-to-all-start.3
  193.5 0.6 dynamic-slice.2
  195.5 95.2 %all-to-all-done.3 = bf16[64,192,64]{1,2,0:T(8,128)(2,1)} async-done(((bf16[64,192,64]{1,2,0:T(8,128)(2,1)}), bf16[64,192,64]{1,2,0:T(8,128)(2,1)}, u32[]{:S(2)}, u32[]{:S(2)}) %all-to-all-start.3) | async-done | bytes 1572896 | tf_op jit(solution)/shard_map/all_to_all | solution.py:81
  290.7 0.6 conditional.4
  291.3 2.3 reshape.365
  293.7 9.9 %all-to-all-start.4 = ((bf16[64,3,4096]{2,1,0:T(4,128)(2,1)}), bf16[64,3,4096]{2,1,0:T(4,128)(2,1)}, u32[]{:S(2)}, u32[]{:S(2)}) async-start(bf16[64,3,4096]{2,1,0:T(4,128)(2,1)} %reshape.365), calls=%async_computation.4 | async-start | bytes 4194304 | tf_op jit(solution)/shard_map/all_to_all | solution.py:105
  304.4 13.0 %all_gather.3 = bf16[16,4096]{1,0:T(8,128)(2,1)S(1)} all-gather(bf16[16,512]{1,0:T(8,128)(2,1)S(1)} %copy-done.17), channel_id=1, replica_groups=mesh['dp'=8,'expert'=64] {'dp'}, dimensions={1}, use_global_device_ids=true | all-gather | bytes 147456 | tf_op jit(solution)/shard_map/all_gather | solution.py:104
  317.4 84.0 %all-to-all-done.4 = bf16[64,3,4096]{2,1,0:T(4,128)(2,1)} async-done(((bf16[64,3,4096]{2,1,0:T(4,128)(2,1)}), bf16[64,3,4096]{2,1,0:T(4,128)(2,1)}, u32[]{:S(2)}, u32[]{:S(2)}) %all-to-all-start.4) | async-done | bytes 1572896 | tf_op jit(solution)/shard_map/all_to_all | solution.py:105
  401.4 3.1 reshape.366
  404.5 1.2 gather_fusion.2
  406.3 2.8 gather_fusion.3
  409.1 2.8 gather.39
  411.9 2.5 select_select_fusion
  414.3 7.4 all-to-all-start.5
  421.8 97.1 %all-to-all-done.5 = bf16[64,3,4096]{2,1,0:T(4,128)(2,1)S(1)} async-done(((bf16[64,3,4096]{2,1,0:T(4,128)(2,1)}), bf16[64,3,4096]{2,1,0:T(4,128)(2,1)S(1)}, u32[]{:S(2)}, u32[]{:S(2)}) %all-to-all-start.5) | async-done | bytes 1572896 | tf_op jit(solution)/shard_map/all_to_all | solution.py:129
  518.8 2.5 reshape.367
  521.3 1.3 conditional.12
  521.3 1.3 broadcast.272
  522.6 9.9 %copy.105 = bf16[1,192,4096]{1,0,2:T(2,128)(2,1)} copy(bf16[1,192,4096]{2,1,0:T(8,128)(2,1)} %bitcast.125) | data formatting | bytes 3145728 | tf_op jit(solution)/shard_map/broadcast_in_dim | solution.py:173
  532.5 24.9 %reduce.15 = bf16[4096,192]{1,0:T(8,128)(2,1)} reduce(bf16[4096,1,192]{2,1,0:T(2,128)(2,1)} %bitcast.116, bf16[]{:T(256)} %broadcast.341), dimensions={1}, to_apply=%bitcast.92.reduce_sub_computation | reduce | bytes 3145730
  557.4 5.5 reshape.476
  563.0 10.6 %all-to-all-start.7 = ((bf16[64,2,6144]{2,1,0:T(2,128)(2,1)}), bf16[64,2,6144]{2,1,0:T(2,128)(2,1)}, u32[]{:S(2)}, u32[]{:S(2)}) async-start(bf16[64,2,6144]{2,1,0:T(2,128)(2,1)} %reshape.476), calls=%async_computation.8 | async-start | bytes 3145728 | tf_op jit(solution)/shard_map/all_to_all | solution.py:173
  574.1 0.7 reduce.13
  575.0 2.5 conditional.5
  575.0 2.5 fusion.41
  577.5 0.6 copy-done.6
  578.1 1.0 select_convert_fusion
  579.1 0.7 reshape.369
  579.9 69.3 %all-to-all-done.7 = bf16[64,2,6144]{2,1,0:T(2,128)(2,1)} async-done(((bf16[64,2,6144]{2,1,0:T(2,128)(2,1)}), bf16[64,2,6144]{2,1,0:T(2,128)(2,1)}, u32[]{:S(2)}, u32[]{:S(2)}) %all-to-all-start.7) | async-done | bytes 1572896 | tf_op jit(solution)/shard_map/all_to_all | solution.py:173
  649.2 7.3 all-to-all-start.6
  656.5 10.7 %reshape.477 = bf16[4096,1,192]{2,1,0:T(2,128)(2,1)} reshape(bf16[64,2,6144]{2,1,0:T(2,128)(2,1)} %all-to-all-done.7) | data formatting | bytes 3145728
  667.1 2.5 copy.115
  669.7 1.7 fusion.14
  671.4 2.5 copy.107
  674.0 15.5 %all-to-all-start.8 = ((bf16[64,192,64]{1,2,0:T(8,128)(2,1)}), bf16[64,192,64]{1,2,0:T(8,128)(2,1)}, u32[]{:S(2)}, u32[]{:S(2)}) async-start(bf16[64,192,64]{1,2,0:T(8,128)(2,1)} %copy.107), calls=%async_computation.9 | async-start | bytes 4194304 | tf_op jit(solution)/shard_map/all_to_all | solution.py:177
  689.7 0.8 broadcast_select_fusion
  690.5 1.6 multiply_reduce_fusion
  692.3 11.3 %psum.7 = f32[16,8]{1,0:T(8,128)S(1)} all-reduce(f32[16,8]{1,0:T(8,128)S(1)} %reduce_sum.100), channel_id=1, replica_groups=mesh['dp'=8,'expert'=64] {'dp'}, use_global_device_ids=true, to_apply=%region_17.18 | all-reduce | flops 128 | bytes 1024 | tf_op jit(solution)/shard_map/psum | solution.py:122
  703.6 0.7 copy.109
  704.3 0.8 gather_fusion.4
  705.2 0.7 fusion.20
  705.9 81.1 %all-to-all-done.8 = bf16[64,192,64]{1,2,0:T(8,128)(2,1)} async-done(((bf16[64,192,64]{1,2,0:T(8,128)(2,1)}), bf16[64,192,64]{1,2,0:T(8,128)(2,1)}, u32[]{:S(2)}, u32[]{:S(2)}) %all-to-all-start.8) | async-done | bytes 1572896 | tf_op jit(solution)/shard_map/all_to_all | solution.py:177
  786.9 4.1 bitcast_convert_fusion
  791.0 5.3 copy.108
  796.4 5.1 fusion.2
  (125 shorter events, 6.1 us)
Async XLA Ops:
  7.2 62.0 %copy-start = (bf16[16,8,192]{2,1,0:T(8,128)(2,1)S(1)}, bf16[16,8,192]{2,1,0:T(8,128)(2,1)}, u32[]{:S(2)}) copy-start(bf16[16,8,192]{2,1,0:T(8,128)(2,1)} %param.14) | copy-start | bytes 147460
  44.5 19.0 %copy-start.29 = (s32[16,8]{0,1:T(8,128)S(1)}, s32[16,8]{0,1:T(8,128)}, u32[]{:S(2)}) copy-start(s32[16,8]{0,1:T(8,128)} %param.18) | copy-start | bytes 1540
  44.5 19.2 %copy-start.30 = (s32[16,8]{0,1:T(8,128)S(1)}, s32[16,8]{0,1:T(8,128)}, u32[]{:S(2)}) copy-start(s32[16,8]{0,1:T(8,128)} %param.19) | copy-start | bytes 1540
  44.5 19.5 %copy-start.35 = (s32[16,2]{0,1:T(2,128)S(1)}, s32[16,2]{0,1:T(2,128)}, u32[]{:S(2)}) copy-start(s32[16,2]{0,1:T(2,128)} %param.20) | copy-start | bytes 388
  44.5 20.2 %copy-start.36 = (s32[64]{0:T(128)S(1)}, s32[64]{0:T(128)}, u32[]{:S(2)}) copy-start(s32[64]{0:T(128)} %param.21) | copy-start | bytes 772
  44.5 95.1 %all-to-all-start.2 = ((bf16[64,2,6144]{2,1,0:T(2,128)(2,1)}), bf16[64,2,6144]{2,1,0:T(2,128)(2,1)S(1)}, u32[]{:S(2)}, u32[]{:S(2)}) async-start(bf16[64,2,6144]{2,1,0:T(2,128)(2,1)} %reshape.474), calls=%async_computation.2 | async-start | bytes 3145728 | tf_op jit(solution)/shard_map/all_to_all | solution.py:77
  63.8 0.6 copy-start.11
  64.1 5.0 copy-start.19
  64.1 5.0 copy-start.27
  64.8 4.3 copy-start.23
  64.8 4.3 copy-start.25
  66.4 2.7 copy-start.18
  68.3 85.4 %copy-start.7 = (pred[64,3]{1,0:T(8,128)(4,1)}, pred[64,3]{1,0:T(8,128)(4,1)S(1)}, u32[]{:S(2)}) copy-start(pred[64,3]{1,0:T(8,128)(4,1)S(1)} %le.50) | copy-start | bytes 580
  70.3 101.7 %copy-start.21 = (s32[64]{0:T(128)}, s32[64]{0:T(128)S(1)}, u32[]{:S(2)}) copy-start(s32[64]{0:T(128)S(1)} %get-tuple-element.144) | copy-start | bytes 772
  139.6 19.4 %all-to-all-start = ((s32[64,1,3]{2,1,0:T(1,128)}), s32[64,1,3]{2,1,0:T(1,128)S(1)}, u32[]{:S(2)}, u32[]{:S(2)}) async-start(s32[64,1,3]{2,1,0:T(1,128)} %bitcast.9), calls=%async_computation | async-start | bytes 65536 | tf_op jit(solution)/shard_map/all_to_all | solution.py:86
  146.5 25.5 %copy-start.32 = (pred[64]{0:T(512)(128)(4,1)}, pred[64]{0:T(512)(128)(4,1)S(1)}, u32[]{:S(2)}) copy-start(pred[64]{0:T(512)(128)(4,1)S(1)} %broadcast_compare_fusion.4) | copy-start | bytes 196
  159.0 27.8 %all-to-all-start.1 = ((bf16[64,3,192]{2,1,0:T(4,128)(2,1)}), bf16[64,3,192]{2,1,0:T(4,128)(2,1)S(1)}, u32[]{:S(2)}, u32[]{:S(2)}) async-start(bf16[64,3,192]{2,1,0:T(4,128)(2,1)} %select_select_fusion.1), calls=%async_computation.1 | async-start | bytes 262144 | tf_op jit(solution)/shard_map/all_to_all | solution.py:85
  176.2 114.5 %copy-start.2 = (bf16[1,192,4096]{2,1,0:T(8,128)(2,1)S(1)}, bf16[1,192,4096]{2,1,0:T(8,128)(2,1)}, u32[]{:S(2)}) copy-start(bf16[1,192,4096]{2,1,0:T(8,128)(2,1)} %param.15) | copy-start | bytes 4718596
  186.8 103.9 %all-to-all-start.3 = ((bf16[64,192,64]{1,2,0:T(8,128)(2,1)}), bf16[64,192,64]{1,2,0:T(8,128)(2,1)}, u32[]{:S(2)}, u32[]{:S(2)}) async-start(bf16[64,192,64]{1,2,0:T(8,128)(2,1)} %copy.97), calls=%async_computation.3 | async-start | bytes 4194304 | tf_op jit(solution)/shard_map/all_to_all | solution.py:81
  293.6 9.9 %copy-start.20 = (s32[128]{0:T(128)S(1)}, s32[128]{0:T(128)}, u32[]{:S(2)}) copy-start(s32[128]{0:T(128)} %copy-done.19) | copy-start | bytes 1540
  293.6 10.0 %copy-start.26 = (s32[128]{0:T(128)S(1)}, s32[128]{0:T(128)}, u32[]{:S(2)}) copy-start(s32[128]{0:T(128)} %copy-done.25) | copy-start | bytes 1540
  293.6 10.1 %copy-start.24 = (s32[128]{0:T(128)S(1)}, s32[128]{0:T(128)}, u32[]{:S(2)}) copy-start(s32[128]{0:T(128)} %copy-done.23) | copy-start | bytes 1540
  293.6 10.2 %copy-start.28 = (s32[128]{0:T(128)S(1)}, s32[128]{0:T(128)}, u32[]{:S(2)}) copy-start(s32[128]{0:T(128)} %copy-done.27) | copy-start | bytes 1540
  293.6 10.3 %copy-start.31 = (f32[16,8]{0,1:T(8,128)S(1)}, f32[16,8]{0,1:T(8,128)}, u32[]{:S(2)}) copy-start(f32[16,8]{0,1:T(8,128)} %param.16) | copy-start | bytes 1540
  293.6 10.5 %copy-start.12 = (s32[16,8]{1,0:T(8,128)S(1)}, s32[16,8]{1,0:T(8,128)}, u32[]{:S(2)}) copy-start(s32[16,8]{1,0:T(8,128)} %copy-done.11) | copy-start | bytes 1540
  293.6 10.7 %copy-start.17 = (bf16[16,512]{1,0:T(8,128)(2,1)S(1)}, bf16[16,512]{1,0:T(8,128)(2,1)}, u32[]{:S(2)}) copy-start(bf16[16,512]{1,0:T(8,128)(2,1)} %param.17) | copy-start | bytes 49156
  293.7 23.7 %copy-start.34 = (s32[128]{0:T(128)S(1)}, s32[128]{0:T(128)}, u32[]{:S(2)}) copy-start(s32[128]{0:T(128)} %get-tuple-element.150) | copy-start | bytes 1540
  293.7 107.7 %all-to-all-start.4 = ((bf16[64,3,4096]{2,1,0:T(4,128)(2,1)}), bf16[64,3,4096]{2,1,0:T(4,128)(2,1)}, u32[]{:S(2)}, u32[]{:S(2)}) async-start(bf16[64,3,4096]{2,1,0:T(4,128)(2,1)} %reshape.365), calls=%async_computation.4 | async-start | bytes 4194304 | tf_op jit(solution)/shard_map/all_to_all | solution.py:105
  304.0 100.5 %copy-start.9 = (f32[16,8]{1,0:T(8,128)}, f32[16,8]{1,0:T(8,128)S(1)}, u32[]{:S(2)}) copy-start(f32[16,8]{1,0:T(8,128)S(1)} %copy.88) | copy-start | bytes 1540
  304.2 100.4 %copy-start.13 = (pred[16,8]{1,0:T(8,128)(4,1)}, pred[16,8]{1,0:T(8,128)(4,1)S(1)}, u32[]{:S(2)}) copy-start(pred[16,8]{1,0:T(8,128)(4,1)S(1)} %get-tuple-element.148) | copy-start | bytes 388
  304.2 100.4 %copy-start.15 = (pred[16,8]{1,0:T(8,128)(4,1)}, pred[16,8]{1,0:T(8,128)(4,1)S(1)}, u32[]{:S(2)}) copy-start(pred[16,8]{1,0:T(8,128)(4,1)S(1)} %get-tuple-element.149) | copy-start | bytes 388
  409.1 2.8 copy-start.8
  414.3 104.5 %all-to-all-start.5 = ((bf16[64,3,4096]{2,1,0:T(4,128)(2,1)}), bf16[64,3,4096]{2,1,0:T(4,128)(2,1)S(1)}, u32[]{:S(2)}, u32[]{:S(2)}) async-start(bf16[64,3,4096]{2,1,0:T(4,128)(2,1)} %select_select_fusion), calls=%async_computation.6 | async-start | bytes 4194304 | tf_op jit(solution)/shard_map/all_to_all | solution.py:129
  563.0 86.2 %all-to-all-start.7 = ((bf16[64,2,6144]{2,1,0:T(2,128)(2,1)}), bf16[64,2,6144]{2,1,0:T(2,128)(2,1)}, u32[]{:S(2)}, u32[]{:S(2)}) async-start(bf16[64,2,6144]{2,1,0:T(2,128)(2,1)} %reshape.476), calls=%async_computation.8 | async-start | bytes 3145728 | tf_op jit(solution)/shard_map/all_to_all | solution.py:173
  577.5 0.6 copy-start.6
  649.2 24.8 %all-to-all-start.6 = ((bf16[64,3,192]{2,1,0:T(4,128)(2,1)}), bf16[64,3,192]{2,1,0:T(4,128)(2,1)S(1)}, u32[]{:S(2)}, u32[]{:S(2)}) async-start(bf16[64,3,192]{2,1,0:T(4,128)(2,1)} %reshape.369), calls=%async_computation.7 | async-start | bytes 262144 | tf_op jit(solution)/shard_map/all_to_all | solution.py:150
  667.1 2.5 copy-start.22
  667.1 2.6 copy-start.33
  674.0 16.6 %copy-start.10 = (f32[16,8]{1,0:T(8,128)S(1)}, f32[16,8]{1,0:T(8,128)}, u32[]{:S(2)}) copy-start(f32[16,8]{1,0:T(8,128)} %copy-done.9) | copy-start | bytes 1540
  674.0 16.6 %copy-start.14 = (pred[16,8]{1,0:T(8,128)(4,1)S(1)}, pred[16,8]{1,0:T(8,128)(4,1)}, u32[]{:S(2)}) copy-start(pred[16,8]{1,0:T(8,128)(4,1)} %copy-done.13) | copy-start | bytes 388
  674.0 16.6 %copy-start.16 = (pred[16,8]{1,0:T(8,128)(4,1)S(1)}, pred[16,8]{1,0:T(8,128)(4,1)}, u32[]{:S(2)}) copy-start(pred[16,8]{1,0:T(8,128)(4,1)} %copy-done.15) | copy-start | bytes 388
  674.0 113.0 %all-to-all-start.8 = ((bf16[64,192,64]{1,2,0:T(8,128)(2,1)}), bf16[64,192,64]{1,2,0:T(8,128)(2,1)}, u32[]{:S(2)}, u32[]{:S(2)}) async-start(bf16[64,192,64]{1,2,0:T(8,128)(2,1)} %copy.107), calls=%async_computation.9 | async-start | bytes 4194304 | tf_op jit(solution)/shard_map/all_to_all | solution.py:177
  689.4 112.1 %reduce-scatter.2.cloned.1.call-start = ((), (), s32[]{:S(2)}) async-start(), calls=%async_computation.10 | async-start | bytes 147456 | tf_op jit(solution)/shard_map/reduce_scatter | solution.py:118
  791.0 5.4 copy-start.5
  791.0 10.5 %copy-start.1 = (bf16[16,8,192]{2,1,0:T(8,128)(2,1)S(1)}, bf16[16,8,192]{2,1,0:T(8,128)(2,1)}, u32[]{:S(2)}) copy-start(bf16[16,8,192]{2,1,0:T(8,128)(2,1)} %param.14) | copy-start | bytes 147460
Sparse Core Ops, SparseCore 0:
  693.6 36.2 reduce-scatter.1
where the time goes:
time: 819 us; the launch traced here: 809 us
  waiting for transfers between devices  508 us (62%)
  starting transfers between devices  96.3 us (12%)
  local copies, waits for them, and re-layouts  89.6 us (11%)
  other arithmetic  63 us (8%)
  blocking collectives  24.3 us (3%)
  between operations  15.6 us (2%)
  matrix products  11.6 us (1%)
    all_to_all x1, waiting for transfers between devices, on_device(): lax.all_to_all(grad_sent, 'expert', split_axis=0, concat_axis=0, tiled=True)  97.1 us
    all_to_all x1, waiting for transfers between devices, on_device(): lax.all_to_all(outgoing, 'expert', split_axis=0, concat_axis=2, tiled=True)  95.2 us
    all_to_all x1, waiting for transfers between devices, on_device(): lax.all_to_all(partial_value.astype(jnp.bfloat16).reshape(n_dev, capacity...  84 us
    all_to_all x1, waiting for transfers between devices, on_device(): lax.all_to_all(homeward, 'expert', split_axis=0, concat_axis=2, tiled=True)  81.1 us
    all_to_all x1, waiting for transfers between devices, on_device(): lax.all_to_all(copy_grad[None], 'expert', split_axis=2, concat_axis=0, ti...  69.3 us
    all_to_all x1, waiting for transfers between devices, on_device(): lax.all_to_all(local_w[None], 'expert', split_axis=2, concat_axis=0, tile...  68.4 us
    unnamed x2, other arithmetic  48.5 us
    unnamed x82, local copies, waits for them, and re-layouts  44.1 us
  transfers between devices with their start and end apart: 10, of which 8 were waited for; matrix products, arithmetic and copies ran while one was open for 8% of the time, Pallas kernels for 0%

commit v1 on v0

--- a/solution.py
+++ b/solution.py
@@ -78,7 +78,12 @@
     outgoing = jnp.einsum("de,ehc->dhc", choose, pieces, preferred_element_type=jnp.float32).astype(
         jnp.bfloat16
     )
-    copy_w = lax.all_to_all(outgoing, "expert", split_axis=0, concat_axis=2, tiled=True)[0]
+    copy_w = jnp.concatenate(
+        lax.all_to_all(
+            jnp.stack(jnp.split(outgoing, lax.axis_size("expert"), axis=0)), "expert", 0, 0
+        ),
+        axis=2,
+    )[0]
     flat_act = activations.reshape(row_count, hidden_part)
     sent = to_slots(flat_act).reshape(n_dev, capacity, hidden_part)
     arrived, arrived_kind = (

time: 819 us -> 864 us (1.055)
  local copies, waits for them, and re-layouts: 89.6 us -> 137 us
    unnamed x82 -> x146, local copies, waits for them, and re-layouts: 44.1 us -> 82.5 us
  transfers between devices with their start and end apart: 10 -> 10, of which waited for: 8 -> 7; matrix products, arithmetic and copies ran while one was open for 8% -> 13% of each run, Pallas kernels for 0% -> 0%
where the time goes in v1:
time: 864 us; the launch traced here: 855 us
  waiting for transfers between devices  509 us (59%)
  local copies, waits for them, and re-layouts  137 us (16%)
  starting transfers between devices  98.8 us (11%)
  other arithmetic  59 us (7%)
  blocking collectives  24.4 us (3%)
  between operations  15.6 us (2%)
  matrix products  11.6 us (1%)
    all_to_all x1, waiting for transfers between devices, on_device(): lax.all_to_all(grad_sent, 'expert', split_axis=0, concat_axis=0, tiled=True)  97.1 us
    all_to_all x1, waiting for transfers between devices, on_device(): lax.all_to_all(jnp.stack(jnp.split(outgoing, lax.axis_size('expert'), axi...  95.2 us
    all_to_all x1, waiting for transfers between devices, on_device(): lax.all_to_all(partial_value.astype(jnp.bfloat16).reshape(n_dev, capacity...  83.7 us
    unnamed x146, local copies, waits for them, and re-layouts  82.5 us
    all_to_all x1, waiting for transfers between devices, on_device(): lax.all_to_all(homeward, 'expert', split_axis=0, concat_axis=2, tiled=True)  81.1 us
    all_to_all x1, waiting for transfers between devices, on_device(): lax.all_to_all(copy_grad[None], 'expert', split_axis=2, concat_axis=0, ti...  69.3 us
    all_to_all x1, waiting for transfers between devices, on_device(): lax.all_to_all(local_w[None], 'expert', split_axis=2, concat_axis=0, tile...  68.5 us
    unnamed x2, other arithmetic  48.6 us
  transfers between devices with their start and end apart: 10, of which 7 were waited for; matrix products, arithmetic and copies ran while one was open for 13% of the time, Pallas kernels for 0%

profile of v1, /device:TPU:14, one launch (start us, length us, event | category | flops | bytes accessed | tf_op | source)
XLA Modules:
  0.0 855.3 jit_solution(6218903319753352295)
XLA Ops:
  7.2 9.9 %copy.2193 = bf16[1,192,4096]{1,0,2:T(2,128)(2,1)} copy(bf16[1,192,4096]{2,1,0:T(8,128)(2,1)} %param.15) | data formatting | bytes 3145728 | tf_op args[1]
  17.6 23.6 %reduce.14 = bf16[4096,192]{1,0:T(8,128)(2,1)S(1)} reduce(bf16[4096,1,192]{2,1,0:T(2,128)(2,1)} %bitcast.243, bf16[]{:T(256)} %broadcast.341), dimensions={1}, to_apply=%bitcast.216.reduce_sub_computation | reduce | bytes 3145730
  41.3 3.3 reshape.477
  44.6 18.9 %all-to-all-start.2 = ((bf16[64,2,6144]{2,1,0:T(2,128)(2,1)}), bf16[64,2,6144]{2,1,0:T(2,128)(2,1)S(1)}, u32[]{:S(2)}, u32[]{:S(2)}) async-start(bf16[64,2,6144]{2,1,0:T(2,128)(2,1)} %reshape.477), calls=%async_computation.2 | async-start | bytes 3145728 | tf_op jit(solution)/shard_map/all_to_all | solution.py:77
  65.5 1.0 scatter_custom_fusion
  66.5 1.6 gather_fusion
  68.4 0.8 select_n.203
  69.2 1.0 gather_fusion.1
  70.4 0.9 select_select_fusion.1
  71.2 68.5 %all-to-all-done.2 = bf16[64,2,6144]{2,1,0:T(2,128)(2,1)S(1)} async-done(((bf16[64,2,6144]{2,1,0:T(2,128)(2,1)}), bf16[64,2,6144]{2,1,0:T(2,128)(2,1)S(1)}, u32[]{:S(2)}, u32[]{:S(2)}) %all-to-all-start.2) | async-done | bytes 1572896 | tf_op jit(solution)/shard_map/all_to_all | solution.py:77
  139.7 7.2 all-to-all-start
  146.9 7.2 reshape.478
  154.1 2.5 copy.2215
  156.7 1.7 fusion.11
  158.8 1.3 fusion.42
  160.0 1.3 fusion.40
  161.4 1.4 fusion.41
  173.1 0.6 constant_dynamic-update-slice_fusion.46
  182.2 0.6 constant_dynamic-update-slice_fusion.31
  200.5 15.1 %all-to-all-start.1 = ((bf16[64,3,192]{2,1,0:T(4,128)(2,1)}), bf16[64,3,192]{2,1,0:T(4,128)(2,1)S(1)}, u32[]{:S(2)}, u32[]{:S(2)}) async-start(bf16[64,3,192]{2,1,0:T(4,128)(2,1)} %select_select_fusion.1), calls=%async_computation.1 | async-start | bytes 262144 | tf_op jit(solution)/shard_map/all_to_all | solution.py:90
  216.8 13.7 %all-to-all-done.1 = bf16[64,3,192]{2,1,0:T(4,128)(2,1)S(1)} async-done(((bf16[64,3,192]{2,1,0:T(4,128)(2,1)}), bf16[64,3,192]{2,1,0:T(4,128)(2,1)S(1)}, u32[]{:S(2)}, u32[]{:S(2)}) %all-to-all-start.1) | async-done | bytes 73760 | tf_op jit(solution)/shard_map/all_to_all | solution.py:90
  230.5 6.7 all-to-all-start.3
  239.2 95.2 %all-to-all-done.3 = bf16[64,1,192,64]{2,3,1,0:T(8,128)(2,1)} async-done(((bf16[64,1,192,64]{2,3,1,0:T(8,128)(2,1)}), bf16[64,1,192,64]{2,3,1,0:T(8,128)(2,1)}, u32[]{:S(2)}, u32[]{:S(2)}) %all-to-all-start.3) | async-done | bytes 1572896 | tf_op jit(solution)/shard_map/all_to_all | solution.py:82
  335.0 2.3 reshape.368
  337.4 10.3 %all-to-all-start.4 = ((bf16[64,3,4096]{2,1,0:T(4,128)(2,1)}), bf16[64,3,4096]{2,1,0:T(4,128)(2,1)}, u32[]{:S(2)}, u32[]{:S(2)}) async-start(bf16[64,3,4096]{2,1,0:T(4,128)(2,1)} %reshape.368), calls=%async_computation.4 | async-start | bytes 4194304 | tf_op jit(solution)/shard_map/all_to_all | solution.py:110
  348.5 13.0 %all_gather.3 = bf16[16,4096]{1,0:T(8,128)(2,1)S(1)} all-gather(bf16[16,512]{1,0:T(8,128)(2,1)S(1)} %copy-done.17), channel_id=1, replica_groups=mesh['dp'=8,'expert'=64] {'dp'}, dimensions={1}, use_global_device_ids=true | all-gather | bytes 147456 | tf_op jit(solution)/shard_map/all_gather | solution.py:109
  361.5 83.7 %all-to-all-done.4 = bf16[64,3,4096]{2,1,0:T(4,128)(2,1)} async-done(((bf16[64,3,4096]{2,1,0:T(4,128)(2,1)}), bf16[64,3,4096]{2,1,0:T(4,128)(2,1)}, u32[]{:S(2)}, u32[]{:S(2)}) %all-to-all-start.4) | async-done | bytes 1572896 | tf_op jit(solution)/shard_map/all_to_all | solution.py:110
  445.3 3.1 reshape.369
  448.4 1.2 gather_fusion.2
  450.2 2.8 gather_fusion.3
  453.0 2.8 gather.39
  455.8 2.5 select_select_fusion
  458.2 7.5 all-to-all-start.5
  465.7 97.1 %all-to-all-done.5 = bf16[64,3,4096]{2,1,0:T(4,128)(2,1)S(1)} async-done(((bf16[64,3,4096]{2,1,0:T(4,128)(2,1)}), bf16[64,3,4096]{2,1,0:T(4,128)(2,1)S(1)}, u32[]{:S(2)}, u32[]{:S(2)}) %all-to-all-start.5) | async-done | bytes 1572896 | tf_op jit(solution)/shard_map/all_to_all | solution.py:134
  562.8 2.5 reshape.370
  565.2 1.3 conditional.12
  565.2 1.3 broadcast.272
  566.6 9.9 %copy.2202 = bf16[1,192,4096]{1,0,2:T(2,128)(2,1)} copy(bf16[1,192,4096]{2,1,0:T(8,128)(2,1)} %bitcast.254) | data formatting | bytes 3145728 | tf_op jit(solution)/shard_map/broadcast_in_dim | solution.py:178
  576.4 25.0 %reduce.15 = bf16[4096,192]{1,0:T(8,128)(2,1)} reduce(bf16[4096,1,192]{2,1,0:T(2,128)(2,1)} %bitcast.244, bf16[]{:T(256)} %broadcast.341), dimensions={1}, to_apply=%bitcast.218.reduce_sub_computation | reduce | bytes 3145730
  601.4 5.5 reshape.479
  607.0 10.6 %all-to-all-start.7 = ((bf16[64,2,6144]{2,1,0:T(2,128)(2,1)}), bf16[64,2,6144]{2,1,0:T(2,128)(2,1)}, u32[]{:S(2)}, u32[]{:S(2)}) async-start(bf16[64,2,6144]{2,1,0:T(2,128)(2,1)} %reshape.479), calls=%async_computation.8 | async-start | bytes 3145728 | tf_op jit(solution)/shard_map/all_to_all | solution.py:178
  618.1 0.7 reduce.13
  619.0 2.5 conditional.5
  619.0 2.5 fusion.45
  622.2 1.0 select_convert_fusion
  623.2 0.7 reshape.372
  623.9 69.3 %all-to-all-done.7 = bf16[64,2,6144]{2,1,0:T(2,128)(2,1)} async-done(((bf16[64,2,6144]{2,1,0:T(2,128)(2,1)}), bf16[64,2,6144]{2,1,0:T(2,128)(2,1)}, u32[]{:S(2)}, u32[]{:S(2)}) %all-to-all-start.7) | async-done | bytes 1572896 | tf_op jit(solution)/shard_map/all_to_all | solution.py:178
  693.2 7.0 all-to-all-start.6
  700.2 10.7 %reshape.480 = bf16[4096,1,192]{2,1,0:T(2,128)(2,1)} reshape(bf16[64,2,6144]{2,1,0:T(2,128)(2,1)} %all-to-all-done.7) | data formatting | bytes 3145728
  710.9 2.5 copy.2281
  713.4 1.7 fusion.14
  715.1 2.5 copy.2204
  717.7 15.4 %all-to-all-start.8 = ((bf16[64,192,64]{1,2,0:T(8,128)(2,1)}), bf16[64,192,64]{1,2,0:T(8,128)(2,1)}, u32[]{:S(2)}, u32[]{:S(2)}) async-start(bf16[64,192,64]{1,2,0:T(8,128)(2,1)} %copy.2204), calls=%async_computation.9 | async-start | bytes 4194304 | tf_op jit(solution)/shard_map/all_to_all | solution.py:182
  733.2 0.8 broadcast_select_fusion
  734.0 1.6 multiply_reduce_fusion
  735.7 11.5 %psum.7 = f32[16,8]{1,0:T(8,128)S(1)} all-reduce(f32[16,8]{1,0:T(8,128)S(1)} %reduce_sum.100), channel_id=1, replica_groups=mesh['dp'=8,'expert'=64] {'dp'}, use_global_device_ids=true, to_apply=%region_17.18 | all-reduce | flops 128 | bytes 1024 | tf_op jit(solution)/shard_map/psum | solution.py:127
  747.2 0.7 copy.2208
  748.0 0.8 gather_fusion.4
  748.8 0.7 fusion.20
  749.5 81.1 %all-to-all-done.8 = bf16[64,192,64]{1,2,0:T(8,128)(2,1)} async-done(((bf16[64,192,64]{1,2,0:T(8,128)(2,1)}), bf16[64,192,64]{1,2,0:T(8,128)(2,1)}, u32[]{:S(2)}, u32[]{:S(2)}) %all-to-all-start.8) | async-done | bytes 1572896 | tf_op jit(solution)/shard_map/all_to_all | solution.py:182
  830.6 2.8 copy.2364
  833.4 4.4 copy.2206
  837.8 5.3 copy.2207
  843.1 5.1 fusion.2
  (192 shorter events, 46.2 us)
Async XLA Ops:
  7.2 62.0 %copy-start = (bf16[16,8,192]{2,1,0:T(8,128)(2,1)S(1)}, bf16[16,8,192]{2,1,0:T(8,128)(2,1)}, u32[]{:S(2)}) copy-start(bf16[16,8,192]{2,1,0:T(8,128)(2,1)} %param.14) | copy-start | bytes 147460
  44.6 19.0 %copy-start.29 = (s32[16,8]{0,1:T(8,128)S(1)}, s32[16,8]{0,1:T(8,128)}, u32[]{:S(2)}) copy-start(s32[16,8]{0,1:T(8,128)} %param.18) | copy-start | bytes 1540
  44.6 19.2 %copy-start.30 = (s32[16,8]{0,1:T(8,128)S(1)}, s32[16,8]{0,1:T(8,128)}, u32[]{:S(2)}) copy-start(s32[16,8]{0,1:T(8,128)} %param.19) | copy-start | bytes 1540
  44.6 19.5 %copy-start.35 = (s32[16,2]{0,1:T(2,128)S(1)}, s32[16,2]{0,1:T(2,128)}, u32[]{:S(2)}) copy-start(s32[16,2]{0,1:T(2,128)} %param.20) | copy-start | bytes 388
  44.6 20.1 %copy-start.36 = (s32[64]{0:T(128)S(1)}, s32[64]{0:T(128)}, u32[]{:S(2)}) copy-start(s32[64]{0:T(128)} %param.21) | copy-start | bytes 772
  44.6 95.1 %all-to-all-start.2 = ((bf16[64,2,6144]{2,1,0:T(2,128)(2,1)}), bf16[64,2,6144]{2,1,0:T(2,128)(2,1)S(1)}, u32[]{:S(2)}, u32[]{:S(2)}) async-start(bf16[64,2,6144]{2,1,0:T(2,128)(2,1)} %reshape.477), calls=%async_computation.2 | async-start | bytes 3145728 | tf_op jit(solution)/shard_map/all_to_all | solution.py:77
  63.9 0.6 copy-start.11
  64.2 4.9 copy-start.19
  64.2 4.9 copy-start.27
  64.9 4.2 copy-start.23
  64.9 4.2 copy-start.25
  66.5 2.7 copy-start.18
  68.4 85.8 %copy-start.7 = (pred[64,3]{1,0:T(8,128)(4,1)}, pred[64,3]{1,0:T(8,128)(4,1)S(1)}, u32[]{:S(2)}) copy-start(pred[64,3]{1,0:T(8,128)(4,1)S(1)} %le.50) | copy-start | bytes 580
  70.3 86.4 %copy-start.21 = (s32[64]{0:T(128)}, s32[64]{0:T(128)S(1)}, u32[]{:S(2)}) copy-start(s32[64]{0:T(128)S(1)} %get-tuple-element.530) | copy-start | bytes 772
  70.4 86.3 %copy-start.32 = (pred[64]{0:T(512)(128)(4,1)}, pred[64]{0:T(512)(128)(4,1)S(1)}, u32[]{:S(2)}) copy-start(pred[64]{0:T(512)(128)(4,1)S(1)} %broadcast_compare_fusion.4) | copy-start | bytes 196
  139.7 60.8 %all-to-all-start = ((s32[64,1,3]{2,1,0:T(1,128)}), s32[64,1,3]{2,1,0:T(1,128)S(1)}, u32[]{:S(2)}, u32[]{:S(2)}) async-start(s32[64,1,3]{2,1,0:T(1,128)} %bitcast.9), calls=%async_computation | async-start | bytes 65536 | tf_op jit(solution)/shard_map/all_to_all | solution.py:91
  200.5 30.0 %all-to-all-start.1 = ((bf16[64,3,192]{2,1,0:T(4,128)(2,1)}), bf16[64,3,192]{2,1,0:T(4,128)(2,1)S(1)}, u32[]{:S(2)}, u32[]{:S(2)}) async-start(bf16[64,3,192]{2,1,0:T(4,128)(2,1)} %select_select_fusion.1), calls=%async_computation.1 | async-start | bytes 262144 | tf_op jit(solution)/shard_map/all_to_all | solution.py:90
  216.8 117.6 %copy-start.2 = (bf16[1,192,4096]{2,1,0:T(8,128)(2,1)S(1)}, bf16[1,192,4096]{2,1,0:T(8,128)(2,1)}, u32[]{:S(2)}) copy-start(bf16[1,192,4096]{2,1,0:T(8,128)(2,1)} %param.15) | copy-start | bytes 4718596
  230.5 103.9 %all-to-all-start.3 = ((bf16[64,1,192,64]{2,3,1,0:T(8,128)(2,1)}), bf16[64,1,192,64]{2,3,1,0:T(8,128)(2,1)}, u32[]{:S(2)}, u32[]{:S(2)}) async-start(bf16[64,1,192,64]{2,3,1,0:T(8,128)(2,1)} %constant_dynamic-update-slice_fusion), calls=%async_computation.3 | async-start | bytes 4194304 | tf_op jit(solution)/shard_map/all_to_all | solution.py:82
  337.3 10.3 %copy-start.20 = (s32[128]{0:T(128)S(1)}, s32[128]{0:T(128)}, u32[]{:S(2)}) copy-start(s32[128]{0:T(128)} %copy-done.19) | copy-start | bytes 1540
  337.3 10.4 %copy-start.26 = (s32[128]{0:T(128)S(1)}, s32[128]{0:T(128)}, u32[]{:S(2)}) copy-start(s32[128]{0:T(128)} %copy-done.25) | copy-start | bytes 1540
  337.3 10.5 %copy-start.24 = (s32[128]{0:T(128)S(1)}, s32[128]{0:T(128)}, u32[]{:S(2)}) copy-start(s32[128]{0:T(128)} %copy-done.23) | copy-start | bytes 1540
  337.3 10.6 %copy-start.28 = (s32[128]{0:T(128)S(1)}, s32[128]{0:T(128)}, u32[]{:S(2)}) copy-start(s32[128]{0:T(128)} %copy-done.27) | copy-start | bytes 1540
  337.3 10.7 %copy-start.31 = (f32[16,8]{0,1:T(8,128)S(1)}, f32[16,8]{0,1:T(8,128)}, u32[]{:S(2)}) copy-start(f32[16,8]{0,1:T(8,128)} %param.16) | copy-start | bytes 1540
  337.4 10.9 %copy-start.12 = (s32[16,8]{1,0:T(8,128)S(1)}, s32[16,8]{1,0:T(8,128)}, u32[]{:S(2)}) copy-start(s32[16,8]{1,0:T(8,128)} %copy-done.11) | copy-start | bytes 1540
  337.4 11.1 %copy-start.17 = (bf16[16,512]{1,0:T(8,128)(2,1)S(1)}, bf16[16,512]{1,0:T(8,128)(2,1)}, u32[]{:S(2)}) copy-start(bf16[16,512]{1,0:T(8,128)(2,1)} %param.17) | copy-start | bytes 49156
  337.4 24.1 %copy-start.34 = (s32[128]{0:T(128)S(1)}, s32[128]{0:T(128)}, u32[]{:S(2)}) copy-start(s32[128]{0:T(128)} %get-tuple-element.536) | copy-start | bytes 1540
  337.4 107.9 %all-to-all-start.4 = ((bf16[64,3,4096]{2,1,0:T(4,128)(2,1)}), bf16[64,3,4096]{2,1,0:T(4,128)(2,1)}, u32[]{:S(2)}, u32[]{:S(2)}) async-start(bf16[64,3,4096]{2,1,0:T(4,128)(2,1)} %reshape.368), calls=%async_computation.4 | async-start | bytes 4194304 | tf_op jit(solution)/shard_map/all_to_all | solution.py:110
  348.1 100.3 %copy-start.9 = (f32[16,8]{1,0:T(8,128)}, f32[16,8]{1,0:T(8,128)S(1)}, u32[]{:S(2)}) copy-start(f32[16,8]{1,0:T(8,128)S(1)} %copy.2187) | copy-start | bytes 1540
  348.3 100.2 %copy-start.13 = (pred[16,8]{1,0:T(8,128)(4,1)}, pred[16,8]{1,0:T(8,128)(4,1)S(1)}, u32[]{:S(2)}) copy-start(pred[16,8]{1,0:T(8,128)(4,1)S(1)} %get-tuple-element.534) | copy-start | bytes 388
  348.3 100.2 %copy-start.15 = (pred[16,8]{1,0:T(8,128)(4,1)}, pred[16,8]{1,0:T(8,128)(4,1)S(1)}, u32[]{:S(2)}) copy-start(pred[16,8]{1,0:T(8,128)(4,1)S(1)} %get-tuple-element.535) | copy-start | bytes 388
  453.0 2.8 copy-start.8
  458.2 104.5 %all-to-all-start.5 = ((bf16[64,3,4096]{2,1,0:T(4,128)(2,1)}), bf16[64,3,4096]{2,1,0:T(4,128)(2,1)S(1)}, u32[]{:S(2)}, u32[]{:S(2)}) async-start(bf16[64,3,4096]{2,1,0:T(4,128)(2,1)} %select_select_fusion), calls=%async_computation.6 | async-start | bytes 4194304 | tf_op jit(solution)/shard_map/all_to_all | solution.py:134
  607.0 86.2 %all-to-all-start.7 = ((bf16[64,2,6144]{2,1,0:T(2,128)(2,1)}), bf16[64,2,6144]{2,1,0:T(2,128)(2,1)}, u32[]{:S(2)}, u32[]{:S(2)}) async-start(bf16[64,2,6144]{2,1,0:T(2,128)(2,1)} %reshape.479), calls=%async_computation.8 | async-start | bytes 3145728 | tf_op jit(solution)/shard_map/all_to_all | solution.py:178
  621.5 0.6 copy-start.6
  693.2 24.5 %all-to-all-start.6 = ((bf16[64,3,192]{2,1,0:T(4,128)(2,1)}), bf16[64,3,192]{2,1,0:T(4,128)(2,1)S(1)}, u32[]{:S(2)}, u32[]{:S(2)}) async-start(bf16[64,3,192]{2,1,0:T(4,128)(2,1)} %reshape.372), calls=%async_computation.7 | async-start | bytes 262144 | tf_op jit(solution)/shard_map/all_to_all | solution.py:155
  710.9 2.5 copy-start.22
  710.9 2.6 copy-start.33
  717.6 16.3 %copy-start.10 = (f32[16,8]{1,0:T(8,128)S(1)}, f32[16,8]{1,0:T(8,128)}, u32[]{:S(2)}) copy-start(f32[16,8]{1,0:T(8,128)} %copy-done.9) | copy-start | bytes 1540
  717.6 16.3 %copy-start.14 = (pred[16,8]{1,0:T(8,128)(4,1)S(1)}, pred[16,8]{1,0:T(8,128)(4,1)}, u32[]{:S(2)}) copy-start(pred[16,8]{1,0:T(8,128)(4,1)} %copy-done.13) | copy-start | bytes 388
  717.7 16.3 %copy-start.16 = (pred[16,8]{1,0:T(8,128)(4,1)S(1)}, pred[16,8]{1,0:T(8,128)(4,1)}, u32[]{:S(2)}) copy-start(pred[16,8]{1,0:T(8,128)(4,1)} %copy-done.15) | copy-start | bytes 388
  717.7 113.0 %all-to-all-start.8 = ((bf16[64,192,64]{1,2,0:T(8,128)(2,1)}), bf16[64,192,64]{1,2,0:T(8,128)(2,1)}, u32[]{:S(2)}, u32[]{:S(2)}) async-start(bf16[64,192,64]{1,2,0:T(8,128)(2,1)} %copy.2204), calls=%async_computation.9 | async-start | bytes 4194304 | tf_op jit(solution)/shard_map/all_to_all | solution.py:182
  733.1 115.1 %reduce-scatter.2.cloned.1.call-start = ((), (), s32[]{:S(2)}) async-start(), calls=%async_computation.10 | async-start | bytes 147456 | tf_op jit(solution)/shard_map/reduce_scatter | solution.py:123
  837.8 5.3 copy-start.5
  837.8 10.4 %copy-start.1 = (bf16[16,8,192]{2,1,0:T(8,128)(2,1)S(1)}, bf16[16,8,192]{2,1,0:T(8,128)(2,1)}, u32[]{:S(2)}) copy-start(bf16[16,8,192]{2,1,0:T(8,128)(2,1)} %param.14) | copy-start | bytes 147460
Sparse Core Ops, SparseCore 0:
  737.3 36.2 reduce-scatter.1
